TPU v7x, 32 devices: a whole 2x2x4 slice. The times are simulated.
32 devices in a mesh: groups: 2 (over x), tm: 16 (over z, y, core).
Axes of the slice: x: 2, y: 2, z: 4, core: 2. Of those that a mesh axis runs over, the one named last changes fastest.
Arguments:
- start_state: float32 [6, 96, 96], P('groups'), parts along dimension 0, may hold values from -0.9 to 0.9
- mobility: float32 [16, 192, 96], P('tm', 'groups'), parts along dimension 1, may hold values from 0.5 to 2
Outputs:
- final_state: float32 [16, 6, 96, 96], P('tm', 'groups'), parts along dimension 1
There are 2 independent parts, one for each index of `groups`. A program takes and returns all parts, laid end to end along the dimension named above; each array names one. Nothing has to cross between parts.
All inputs are finite; a program needn't handle non-finite values.
Results may differ from a plain program's by a relative error of at most 0.00029.
Values sent between devices are 32-bit elements; how exact they have to be, the bound alone decides.
A program may use at most 128 MiB of HBM per device.

v0:
```python
import functools

import jax
import jax.numpy as jnp
import ml_dtypes
import numpy as np
from jax import lax
from jax.experimental import pallas as pl
from jax.experimental.pallas import tpu as pltpu
from jax.sharding import PartitionSpec as P

DT = 0.015
KAPPA = 1.0
ETA = 0.5
DE = 0.5
GAMMA = 2.0
M1 = 0.6
M2 = -0.4
MEAN = 1.0
LANES = 128
ROWS = 8
PER = 1
F32 = jnp.float32
BF16 = jnp.bfloat16


def split(matrix):
    high = matrix.astype(ml_dtypes.bfloat16)
    low = (matrix - high.astype(np.float64)).astype(ml_dtypes.bfloat16)
    return high, low


def constants(grid):
    half = grid // 2
    tiles = half // 4
    rows = tiles * ROWS
    wave = np.arange(half)
    angle = 2.0 * np.pi * np.outer(wave, wave) / half
    basis = (np.cos(angle) + np.sin(angle)) / np.sqrt(half)
    mean = 0.5 * np.repeat(basis, 2, axis=1)
    spread = np.repeat(basis, 2, axis=0)
    edge = (LANES - grid) // 2
    lane = np.arange(LANES)
    column = np.where(lane < grid, lane, np.where(lane < grid + edge, lane - grid, lane - 2 * edge))
    left = np.zeros((2 * rows, 3 * grid))
    right = np.zeros((2 * LANES, LANES))
    back_right = np.zeros((LANES, 2 * LANES))
    back_left = np.zeros((3 * grid, 2 * rows))
    square = np.sin(np.pi * wave / half) ** 2
    step = np.zeros((4, rows, LANES))
    for s in range(2):
        right[s * LANES : s * LANES + grid, s * half : (s + 1) * half] = mean.T
        back_right[s * half : (s + 1) * half, s * LANES : (s + 1) * LANES] = spread[column].T
        lanes = slice(s * half, (s + 1) * half)
        for j in range(tiles):
            for h in range(2):
                a = 4 * j + 2 * h + s
                sym = -(square[a] + square)
                for f in range(3):
                    row = ROWS * j + 2 * f + h
                    left[s * rows + row, f * grid : (f + 1) * grid] = mean[a]
                    back_left[f * grid : (f + 1) * grid, s * rows + row] = spread[:, a]
                row = ROWS * j + h
                step[0, row, lanes] = MEAN * (-sym - KAPPA * sym * sym)
                step[1, row, lanes] = MEAN * ETA * sym
                step[2, row, lanes] = MEAN * ETA * sym
                step[0, row + 2, lanes] = DE * sym - GAMMA
                step[0, row + 4, lanes] = DE * sym - GAMMA
                step[3, row + 2, lanes] = GAMMA * M1
                step[2, row + 4, lanes] = GAMMA * M2
    step = (DT * step).astype(np.float32).reshape(4, tiles, ROWS, LANES)
    pieces = []
    for matrix in (left, right, back_right, back_left):
        pieces.extend(split(matrix))
    return pieces + [step]


def product_left(pair, x):
    high_c, low_c = pair
    high = x.astype(BF16)
    low = (x - high.astype(F32)).astype(BF16)
    dot = functools.partial(jnp.dot, preferred_element_type=F32)
    return dot(high_c, high) + (dot(high_c, low) + dot(low_c, high))


def product_right(x, pair):
    high_c, low_c = pair
    high = x.astype(BF16)
    low = (x - high.astype(F32)).astype(BF16)
    dot = functools.partial(jnp.dot, preferred_element_type=F32)
    return dot(high, high_c) + (dot(low, high_c) + dot(high, low_c))


def up(x):
    return pltpu.roll(x, x.shape[0] - 1, 0)


def down(x):
    return pltpu.roll(x, 1, 0)


def west(x):
    return pltpu.roll(x, LANES - 1, 1)


def east(x):
    return pltpu.roll(x, 1, 1)


def laplace(x):
    return (up(x) + down(x)) + (west(x) + east(x)) - 4.0 * x


def fine_rate(state, face_x, face_y):
    c, one, two = state
    mu = c * c * c - c - KAPPA * laplace(c) + ETA * (one + two)
    jx = face_x * (up(mu) - mu)
    jy = face_y * (west(mu) - mu)
    rate_c = (jx - down(jx)) + (jy - east(jy))
    rate_one = DE * laplace(one) - GAMMA * (one - M1 * c)
    rate_two = DE * laplace(two) - GAMMA * (two - M2 * c)
    return rate_c, rate_one, rate_two


def combine(*terms):
    total = None
    for weight, state in terms:
        part = state if weight == 1.0 else tuple(weight * x for x in state)
        total = part if total is None else tuple(a + b for a, b in zip(total, part))
    return total


def block_mean(state):
    out = []
    for x in state:
        rows, lanes = x.shape
        lane = lax.broadcasted_iota(jnp.int32, x.shape, 1)
        row = lax.broadcasted_iota(jnp.int32, x.shape, 0)
        x = x + jnp.where(lane % 2 == 0, west(x), east(x))
        x = x + jnp.where(row % 2 == 0, up(x), down(x))
        out.append(0.25 * x)
    return tuple(out)


def mode_rate(step, modes):
    axis = modes.ndim - 2
    return (
        step[0] * modes
        + step[1] * pltpu.roll(modes, ROWS - 2, axis)
        + step[2] * pltpu.roll(modes, 4, axis)
        + step[3] * pltpu.roll(modes, 2, axis)
    )


def kernel(
    n, scanners,
    start_ref, mob_ref, lh, ll, rh, rl, brh, brl, blh, bll, step_ref,
    out_ref,
    wide, fluct, arrived, modes, gathered, results, returned,
    w_send, w_recv, send_one, recv_one, send_two, recv_two,
):
    me = lax.axis_index("tm")
    grid = mob_ref.shape[-1]
    edge = (LANES - grid) // 2
    tiles = step_ref.shape[1]
    count = len(scanners)
    per = tiles // count
    MESH = pl.DeviceIdType.MESH

    barrier = pltpu.get_barrier_semaphore()

    def greet(k, carry):
        other = lax.rem(me + k, n)
        pl.semaphore_signal(barrier, inc=1, device_id={"tm": other}, device_id_type=MESH)
        return carry

    lax.fori_loop(1, n, greet, 0)

    lane = lax.broadcasted_iota(jnp.int32, (grid, LANES), 1)

    def widen(x, slot):
        wide[slot, :, :grid] = x
        x = wide[slot]
        return jnp.where(
            lane < grid,
            x,
            jnp.where(lane < grid + edge, pltpu.roll(x, grid, 1), pltpu.roll(x, 2 * edge, 1)),
        )

    mob = widen(mob_ref[0], 3)
    face_x = 0.5 * (mob + up(mob))
    face_y = 0.5 * (mob + west(mob))
    rate = lambda state: fine_rate(state, face_x, face_y)

    def forward(state):
        x = jnp.concatenate(state, axis=0)
        rows = tiles * ROWS
        g = product_left((lh[...], ll[...]), x)
        g = jnp.concatenate([g[:rows], g[rows:]], axis=1)
        return product_right(g, (rh[...], rl[...])).reshape(tiles, ROWS, LANES)

    def inverse(parts):
        rows = tiles * ROWS
        x = jnp.concatenate([p.reshape(rows, LANES) for p in parts], axis=0)
        z = product_right(x, (brh[...], brl[...]))
        z = jnp.concatenate(
            [
                jnp.concatenate([z[k * rows : (k + 1) * rows, s * LANES : (s + 1) * LANES] for k in range(len(parts))], axis=1)
                for s in range(2)
            ],
            axis=0,
        )
        y = product_left((blh[...], bll[...]), z)
        return [
            tuple(y[f * grid : (f + 1) * grid, k * LANES : (k + 1) * LANES] for f in range(3))
            for k in range(len(parts))
        ]

    step = [step_ref[k] for k in range(4)]

    def remote(src, dst, send, recv, target):
        return pltpu.make_async_remote_copy(
            src_ref=src, dst_ref=dst, send_sem=send, recv_sem=recv,
            device_id={"tm": target}, device_id_type=MESH,
        )

    def drain(ref, sem):
        pltpu.make_async_copy(ref, ref, sem).wait()

    def is_scanner():
        hit = me == scanners[0]
        for d in scanners[1:]:
            hit = jnp.logical_or(hit, me == d)
        return hit

    def scan(it, start_modes_ref, offsets, inclusive):
        modes[it] = offsets
        for s, d in enumerate(scanners):
            @pl.when(me != d)
            def _():
                remote(
                    modes.at[it, pl.ds(s * per, per)], gathered.at[it, me],
                    send_one.at[it], recv_one.at[it], d,
                ).start()
        for s, d in enumerate(scanners):
            @pl.when(me == d)
            def _():
                mine = [step_ref[k, s * per : (s + 1) * per] for k in range(4)]
                state = start_modes_ref[s * per : (s + 1) * per]
                gathered[it, d] = modes[it, s * per : (s + 1) * per]
                drain(gathered.at[it, pl.ds(0, n - 1)], recv_one.at[it])
                for k in range(n):
                    after = None
                    if inclusive or k + 1 < n:
                        after = state + (mode_rate(mine, state) + gathered[it, k])
                    value = after if inclusive else state
                    results[it, k] = value
                    if k == d:
                        returned[it, s * per : (s + 1) * per] = value
                    else:
                        remote(
                            results.at[it, k], returned.at[it, pl.ds(s * per, per)],
                            send_two.at[it], recv_two.at[it], k,
                        ).start()
                    state = after

    def scanned(it):
        one_of = is_scanner()

        @pl.when(one_of)
        def _():
            drain(returned.at[it, pl.ds(0, (count - 1) * per)], recv_two.at[it])

        @pl.when(jnp.logical_not(one_of))
        def _():
            drain(returned.at[it], recv_two.at[it])

        return returned[it]

    u0 = tuple(widen(start_ref[f], f) for f in range(3))
    f0 = rate(u0)
    u1 = combine((1.0, u0), (0.5 * DT, f0))
    a1 = rate(u1)
    w = combine((1.0, u1), (0.5 * DT, a1))
    pw = block_mean(w)
    wf = combine((1.0, w), (-1.0, pw))
    for f in range(3):
        fluct[f] = wf[f]
    start_modes = forward(u0)
    modes[2] = start_modes
    pl.semaphore_wait(barrier, n - 1)

    @pl.when(me + 1 < n)
    def _():
        remote(fluct, arrived, w_send, w_recv, me + 1).start()

    a2 = rate(w)
    integral = combine((DT / 6.0, f0), (DT * 2.0 / 3.0, a1), (DT / 6.0, a2))
    offsets = forward(integral) - mode_rate(step, start_modes)
    scan(0, modes.at[2], offsets, False)

    p0 = block_mean(u0)
    u1f = combine((1.0, u1), (-0.5, p0), (-0.5, pw))

    @pl.when(me == 0)
    def _():
        for f in range(3):
            arrived[f] = u0[f] - p0[f]

    begin = scanned(0)
    end = begin + (mode_rate(step, begin) + offsets)
    pb, pe = inverse([begin, end])

    @pl.when(me > 0)
    def _():
        drain(arrived, w_recv)

    u0 = tuple(arrived[f] + pb[f] for f in range(3))
    u1 = combine((1.0, u1f), (0.5, pb), (0.5, pe))
    u2 = combine((1.0, wf), (1.0, pe))
    f1 = rate(u1)
    f2 = rate(u2)
    a0 = rate(u0)
    u1 = combine(
        (1.0, u0), (0.5 * DT, a0), (DT * (5.0 / 24.0 - 0.5), f0), (DT / 3.0, f1), (-DT / 24.0, f2)
    )
    a1 = rate(u1)
    w = combine(
        (1.0, u1), (0.5 * DT, a1), (-DT / 24.0, f0), (DT * (1.0 / 3.0 - 0.5), f1), (DT * 5.0 / 24.0, f2)
    )
    a2 = rate(w)
    integral = combine((DT / 6.0, a0), (DT * 2.0 / 3.0, a1), (DT / 6.0, a2))
    offsets = forward(integral) - mode_rate(step, begin)
    scan(1, modes.at[2], offsets, True)
    pw = block_mean(w)
    wf = combine((1.0, w), (-1.0, pw))
    for f in range(3):
        wide[f] = wf[f]
    (pe,) = inverse([scanned(1)])
    for f in range(3):
        out_ref[0, f] = (wide[f] + pe[f])[:, :grid]

    @pl.when(me + 1 < n)
    def _():
        drain(fluct, w_send)

    one_of = is_scanner()
    for it in range(2):
        @pl.when(one_of)
        def _():
            drain(modes.at[it, pl.ds(0, (count - 1) * per)], send_one.at[it])
            drain(results.at[it, pl.ds(0, n - 1)], send_two.at[it])

        @pl.when(jnp.logical_not(one_of))
        def _():
            drain(modes.at[it], send_one.at[it])


def local(n, start_state, mobility):
    grid = start_state.shape[-1]
    made = constants(grid)
    tiles = made[-1].shape[1]
    count = tiles // PER
    scanners = tuple(s * n // count for s in range(count))
    return pl.pallas_call(
        functools.partial(kernel, n, scanners),
        out_shape=jax.ShapeDtypeStruct((1,) + start_state.shape, F32),
        in_specs=[pl.BlockSpec(memory_space=pltpu.VMEM)] * (2 + len(made)),
        out_specs=pl.BlockSpec(memory_space=pltpu.VMEM),
        scratch_shapes=[
            pltpu.VMEM((4, grid, LANES), F32),
            pltpu.VMEM((3, grid, LANES), F32),
            pltpu.VMEM((3, grid, LANES), F32),
            pltpu.VMEM((3, tiles, ROWS, LANES), F32),
            pltpu.VMEM((2, n, PER, ROWS, LANES), F32),
            pltpu.VMEM((2, n, PER, ROWS, LANES), F32),
            pltpu.VMEM((2, tiles, ROWS, LANES), F32),
            pltpu.SemaphoreType.DMA,
            pltpu.SemaphoreType.DMA,
            pltpu.SemaphoreType.DMA((2,)),
            pltpu.SemaphoreType.DMA((2,)),
            pltpu.SemaphoreType.DMA((2,)),
            pltpu.SemaphoreType.DMA((2,)),
        ],
        compiler_params=pltpu.CompilerParams(
            collective_id=0, has_side_effects=True, vmem_limit_bytes=40 * 1024 * 1024
        ),
        cost_estimate=pl.CostEstimate(flops=200_000_000, bytes_accessed=1_500_000, transcendentals=0),
    )(start_state, mobility, *[jnp.asarray(m) for m in made])


def solution(mesh):
    n = mesh.shape["tm"]
    in_specs = (P("groups", None, None), P("tm", "groups", None))
    out_specs = P("tm", "groups", None, None)
    return jax.shard_map(
        functools.partial(local, n), mesh=mesh, in_specs=in_specs, out_specs=out_specs, check_vma=False
    )
```

profile of v0, /device:TPU:0, one launch (start us, length us, event | category | flops | bytes accessed | tf_op | source)
XLA Modules:
  0.0 36.1 jit_solution(8540973764027321571)
XLA Ops:
  0.0 0.0 copy-start
  0.0 0.9 %copy-done = f32[4,12,8,128]{3,2,1,0:T(8,128)S(1)} copy-done((f32[4,12,8,128]{3,2,1,0:T(8,128)S(1)}, f32[4,12,8,128]{3,2,1,0:T(8,128)}, u32[]{:S(2)}) %copy-start) | copy-done | bytes 196632
  0.9 0.0 copy-start.1
  0.9 0.9 %copy-done.1 = f32[3,96,96]{2,1,0:T(8,128)S(1)} copy-done((f32[3,96,96]{2,1,0:T(8,128)S(1)}, f32[3,96,96]{2,1,0:T(8,128)}, u32[]{:S(2)}) %copy-start.1) | copy-done | bytes 110616
  1.8 0.0 copy-start.2
  1.8 0.9 %copy-done.2 = bf16[288,192]{1,0:T(8,128)(2,1)S(1)} copy-done((bf16[288,192]{1,0:T(8,128)(2,1)S(1)}, bf16[288,192]{1,0:T(8,128)(2,1)}, u32[]{:S(2)}) %copy-start.2) | copy-done | bytes 110616
  2.7 0.0 copy-start.3
  2.8 0.9 %copy-done.3 = bf16[288,192]{1,0:T(8,128)(2,1)S(1)} copy-done((bf16[288,192]{1,0:T(8,128)(2,1)S(1)}, bf16[288,192]{1,0:T(8,128)(2,1)}, u32[]{:S(2)}) %copy-start.3) | copy-done | bytes 110616
  3.7 0.0 copy-start.4
  3.7 0.9 %copy-done.4 = bf16[192,288]{1,0:T(8,128)(2,1)S(1)} copy-done((bf16[192,288]{1,0:T(8,128)(2,1)S(1)}, bf16[192,288]{1,0:T(8,128)(2,1)}, u32[]{:S(2)}) %copy-start.4) | copy-done | bytes 110616
  4.6 0.0 copy-start.5
  4.6 0.9 %copy-done.5 = bf16[192,288]{1,0:T(8,128)(2,1)S(1)} copy-done((bf16[192,288]{1,0:T(8,128)(2,1)S(1)}, bf16[192,288]{1,0:T(8,128)(2,1)}, u32[]{:S(2)}) %copy-start.5) | copy-done | bytes 110616
  5.5 0.0 copy-start.6
  5.5 0.8 %copy-done.6 = bf16[128,256]{1,0:T(8,128)(2,1)S(1)} copy-done((bf16[128,256]{1,0:T(8,128)(2,1)S(1)}, bf16[128,256]{1,0:T(8,128)(2,1)}, u32[]{:S(2)}) %copy-start.6) | copy-done | bytes 65560
  6.3 0.0 copy-start.7
  6.3 0.8 %copy-done.7 = bf16[128,256]{1,0:T(8,128)(2,1)S(1)} copy-done((bf16[128,256]{1,0:T(8,128)(2,1)S(1)}, bf16[128,256]{1,0:T(8,128)(2,1)}, u32[]{:S(2)}) %copy-start.7) | copy-done | bytes 65560
  7.2 0.0 copy-start.8
  7.2 0.8 %copy-done.8 = bf16[256,128]{1,0:T(8,128)(2,1)S(1)} copy-done((bf16[256,128]{1,0:T(8,128)(2,1)S(1)}, bf16[256,128]{1,0:T(8,128)(2,1)}, u32[]{:S(2)}) %copy-start.8) | copy-done | bytes 65560
  8.0 0.0 copy-start.9
  8.0 0.8 %copy-done.9 = bf16[256,128]{1,0:T(8,128)(2,1)S(1)} copy-done((bf16[256,128]{1,0:T(8,128)(2,1)S(1)}, bf16[256,128]{1,0:T(8,128)(2,1)}, u32[]{:S(2)}) %copy-start.9) | copy-done | bytes 65560
  8.8 0.0 copy-start.10
  8.8 0.8 %copy-done.10 = f32[1,96,96]{2,1,0:T(8,128)S(1)} copy-done((f32[1,96,96]{2,1,0:T(8,128)S(1)}, f32[1,96,96]{2,1,0:T(8,128)}, u32[]{:S(2)}) %copy-start.10) | copy-done | bytes 36888
  9.6 25.8 %shard_map.109 = f32[1,3,96,96]{3,2,1,0:T(8,128)S(1)} custom-call(f32[3,96,96]{2,1,0:T(8,128)S(1)} %copy-done.1, f32[1,96,96]{2,1,0:T(8,128)S(1)} %copy-done.10, bf16[192,288]{1,0:T(8,128)(2,1)S(1)} %copy-done.5, bf16[192,288]{1,0:T(8,128)(2,1)S(1)} %copy-done.4, bf16[256,128]{1,0:T(8,128)(2,1)S(1)} %copy-done.9, bf16[256,128]{1,0:T(8,128)(2,1)S(1)} %copy-done.8, ...), custom_call_target="tpu_custom_call" | custom-call | flops 200000000 | bytes 1500000 | tf_op jit(solution)/shard_map/pallas_call | solution.py:365
  35.4 0.7 %copy.13 = f32[1,3,96,96]{3,2,1,0:T(8,128)} copy(f32[1,3,96,96]{3,2,1,0:T(8,128)S(1)} %shard_map.109) | data formatting | bytes 221184
Async XLA Ops:
  0.0 0.9 %copy-start = (f32[4,12,8,128]{3,2,1,0:T(8,128)S(1)}, f32[4,12,8,128]{3,2,1,0:T(8,128)}, u32[]{:S(2)}) copy-start(f32[4,12,8,128]{3,2,1,0:T(8,128)} %constant.26.clone.step_ref) | copy-start | bytes 589828
  0.9 0.9 %copy-start.1 = (f32[3,96,96]{2,1,0:T(8,128)S(1)}, f32[3,96,96]{2,1,0:T(8,128)}, u32[]{:S(2)}) copy-start(f32[3,96,96]{2,1,0:T(8,128)} %start_ref.1) | copy-start | bytes 331780
  1.8 0.9 %copy-start.2 = (bf16[288,192]{1,0:T(8,128)(2,1)S(1)}, bf16[288,192]{1,0:T(8,128)(2,1)}, u32[]{:S(2)}) copy-start(bf16[288,192]{1,0:T(8,128)(2,1)} %constant.25.clone.bll) | copy-start | bytes 331780
  2.7 0.9 %copy-start.3 = (bf16[288,192]{1,0:T(8,128)(2,1)S(1)}, bf16[288,192]{1,0:T(8,128)(2,1)}, u32[]{:S(2)}) copy-start(bf16[288,192]{1,0:T(8,128)(2,1)} %constant.24.clone.blh) | copy-start | bytes 331780
  3.7 0.9 %copy-start.4 = (bf16[192,288]{1,0:T(8,128)(2,1)S(1)}, bf16[192,288]{1,0:T(8,128)(2,1)}, u32[]{:S(2)}) copy-start(bf16[192,288]{1,0:T(8,128)(2,1)} %constant.19.clone.ll) | copy-start | bytes 331780
  4.6 0.9 %copy-start.5 = (bf16[192,288]{1,0:T(8,128)(2,1)S(1)}, bf16[192,288]{1,0:T(8,128)(2,1)}, u32[]{:S(2)}) copy-start(bf16[192,288]{1,0:T(8,128)(2,1)} %constant.18.clone.lh) | copy-start | bytes 331780
  5.5 0.8 %copy-start.6 = (bf16[128,256]{1,0:T(8,128)(2,1)S(1)}, bf16[128,256]{1,0:T(8,128)(2,1)}, u32[]{:S(2)}) copy-start(bf16[128,256]{1,0:T(8,128)(2,1)} %constant.23.clone.brl) | copy-start | bytes 196612
  6.3 0.8 %copy-start.7 = (bf16[128,256]{1,0:T(8,128)(2,1)S(1)}, bf16[128,256]{1,0:T(8,128)(2,1)}, u32[]{:S(2)}) copy-start(bf16[128,256]{1,0:T(8,128)(2,1)} %constant.22.clone.brh) | copy-start | bytes 196612
  7.2 0.8 %copy-start.8 = (bf16[256,128]{1,0:T(8,128)(2,1)S(1)}, bf16[256,128]{1,0:T(8,128)(2,1)}, u32[]{:S(2)}) copy-start(bf16[256,128]{1,0:T(8,128)(2,1)} %constant.21.clone.rl) | copy-start | bytes 196612
  8.0 0.8 %copy-start.9 = (bf16[256,128]{1,0:T(8,128)(2,1)S(1)}, bf16[256,128]{1,0:T(8,128)(2,1)}, u32[]{:S(2)}) copy-start(bf16[256,128]{1,0:T(8,128)(2,1)} %constant.20.clone.rh) | copy-start | bytes 196612
  8.8 0.8 %copy-start.10 = (f32[1,96,96]{2,1,0:T(8,128)S(1)}, f32[1,96,96]{2,1,0:T(8,128)}, u32[]{:S(2)}) copy-start(f32[1,96,96]{2,1,0:T(8,128)} %mob_ref.1) | copy-start | bytes 110596
where the time goes:
time: 36.6 us; the launch traced here: 36.1 us
  Pallas kernels  25.8 us (70%)
  local copies, waits for them, and re-layouts  10.3 us (28%)
    pallas_call x1, Pallas kernels, local(): pl.pallas_call(functools.partial(kernel, n, scanners), out_shape=jax.Shap...  25.8 us
    unnamed x23, local copies, waits for them, and re-layouts  10.3 us

commit v1 on v0

--- a/solution.py
+++ b/solution.py
@@ -69,10 +69,7 @@
                 step[3, row + 2, lanes] = GAMMA * M1
                 step[2, row + 4, lanes] = GAMMA * M2
     step = (DT * step).astype(np.float32).reshape(4, tiles, ROWS, LANES)
-    pieces = []
-    for matrix in (left, right, back_right, back_left):
-        pieces.extend(split(matrix))
-    return pieces + [step]
+    return [np.stack(split(matrix)) for matrix in (left, right, back_right, back_left)] + [step]
 
 
 def product_left(pair, x):
@@ -154,8 +151,9 @@
 
 def kernel(
     n, scanners,
-    start_ref, mob_ref, lh, ll, rh, rl, brh, brl, blh, bll, step_ref,
+    start_hbm, mob_hbm, left_hbm, right_hbm, back_right_hbm, back_left_hbm, step_hbm,
     out_ref,
+    start_ref, mob_ref, left_ref, right_ref, back_right_ref, back_left_ref, step_ref, loaded,
     wide, fluct, arrived, modes, gathered, results, returned,
     w_send, w_recv, send_one, recv_one, send_two, recv_two,
 ):
@@ -167,6 +165,22 @@
     per = tiles // count
     MESH = pl.DeviceIdType.MESH
 
+    loads = [
+        pltpu.make_async_copy(src, dst, loaded.at[k])
+        for k, (src, dst) in enumerate(
+            [
+                (start_hbm, start_ref),
+                (mob_hbm, mob_ref),
+                (left_hbm, left_ref),
+                (right_hbm, right_ref),
+                (step_hbm, step_ref),
+                (back_right_hbm, back_right_ref),
+                (back_left_hbm, back_left_ref),
+            ]
+        )
+    ]
+    for load in loads:
+        load.start()
     barrier = pltpu.get_barrier_semaphore()
 
     def greet(k, carry):
@@ -187,6 +201,7 @@
             jnp.where(lane < grid + edge, pltpu.roll(x, grid, 1), pltpu.roll(x, 2 * edge, 1)),
         )
 
+    loads[1].wait()
     mob = widen(mob_ref[0], 3)
     face_x = 0.5 * (mob + up(mob))
     face_y = 0.5 * (mob + west(mob))
@@ -195,14 +210,14 @@
     def forward(state):
         x = jnp.concatenate(state, axis=0)
         rows = tiles * ROWS
-        g = product_left((lh[...], ll[...]), x)
+        g = product_left((left_ref[0], left_ref[1]), x)
         g = jnp.concatenate([g[:rows], g[rows:]], axis=1)
-        return product_right(g, (rh[...], rl[...])).reshape(tiles, ROWS, LANES)
+        return product_right(g, (right_ref[0], right_ref[1])).reshape(tiles, ROWS, LANES)
 
     def inverse(parts):
         rows = tiles * ROWS
         x = jnp.concatenate([p.reshape(rows, LANES) for p in parts], axis=0)
-        z = product_right(x, (brh[...], brl[...]))
+        z = product_right(x, (back_right_ref[0], back_right_ref[1]))
         z = jnp.concatenate(
             [
                 jnp.concatenate([z[k * rows : (k + 1) * rows, s * LANES : (s + 1) * LANES] for k in range(len(parts))], axis=1)
@@ -210,13 +225,11 @@
             ],
             axis=0,
         )
-        y = product_left((blh[...], bll[...]), z)
+        y = product_left((back_left_ref[0], back_left_ref[1]), z)
         return [
             tuple(y[f * grid : (f + 1) * grid, k * LANES : (k + 1) * LANES] for f in range(3))
             for k in range(len(parts))
         ]
-
-    step = [step_ref[k] for k in range(4)]
 
     def remote(src, dst, send, recv, target):
         return pltpu.make_async_remote_copy(
@@ -277,6 +290,7 @@
 
         return returned[it]
 
+    loads[0].wait()
     u0 = tuple(widen(start_ref[f], f) for f in range(3))
     f0 = rate(u0)
     u1 = combine((1.0, u0), (0.5 * DT, f0))
@@ -286,6 +300,9 @@
     wf = combine((1.0, w), (-1.0, pw))
     for f in range(3):
         fluct[f] = wf[f]
+    for k in (2, 3, 4):
+        loads[k].wait()
+    step = [step_ref[k] for k in range(4)]
     start_modes = forward(u0)
     modes[2] = start_modes
     pl.semaphore_wait(barrier, n - 1)
@@ -307,6 +324,8 @@
         for f in range(3):
             arrived[f] = u0[f] - p0[f]
 
+    for k in (5, 6):
+        loads[k].wait()
     begin = scanned(0)
     end = begin + (mode_rate(step, begin) + offsets)
     pb, pe = inverse([begin, end])
@@ -365,9 +384,11 @@
     return pl.pallas_call(
         functools.partial(kernel, n, scanners),
         out_shape=jax.ShapeDtypeStruct((1,) + start_state.shape, F32),
-        in_specs=[pl.BlockSpec(memory_space=pltpu.VMEM)] * (2 + len(made)),
+        in_specs=[pl.BlockSpec(memory_space=pl.ANY)] * (2 + len(made)),
         out_specs=pl.BlockSpec(memory_space=pltpu.VMEM),
-        scratch_shapes=[
+        scratch_shapes=[pltpu.VMEM(x.shape, x.dtype) for x in (start_state, mobility, *made)]
+        + [
+            pltpu.SemaphoreType.DMA((2 + len(made),)),
             pltpu.VMEM((4, grid, LANES), F32),
             pltpu.VMEM((3, grid, LANES), F32),
             pltpu.VMEM((3, grid, LANES), F32),
@@ -383,7 +404,7 @@
             pltpu.SemaphoreType.DMA((2,)),
         ],
         compiler_params=pltpu.CompilerParams(
-            collective_id=0, has_side_effects=True, vmem_limit_bytes=40 * 1024 * 1024
+            collective_id=0, has_side_effects=True, vmem_limit_bytes=60 * 1024 * 1024
         ),
         cost_estimate=pl.CostEstimate(flops=200_000_000, bytes_accessed=1_500_000, transcendentals=0),
     )(start_state, mobility, *[jnp.asarray(m) for m in made])

time: 36.6 us -> 28.3 us (0.77)
  local copies, waits for them, and re-layouts: 10.3 us -> 1.58 us
  Pallas kernels: 25.8 us -> 26.5 us
    unnamed x23 -> x1, local copies, waits for them, and re-layouts: 10.3 us -> 1.58 us
    pallas_call x1, Pallas kernels: 25.8 us -> 26.5 us  [local(): pl.pallas_call(functools.partial(kernel, n, scanners), out_shape=jax.Shap...]
where the time goes in v1:
time: 28.3 us; the launch traced here: 28.1 us
  Pallas kernels  26.5 us (94%)
  local copies, waits for them, and re-layouts  1.58 us (6%)
    pallas_call x1, Pallas kernels, local(): pl.pallas_call(functools.partial(kernel, n, scanners), out_shape=jax.Shap...  26.5 us
    unnamed x1, local copies, waits for them, and re-layouts  1.58 us

profile of v1, /device:TPU:0, one launch (start us, length us, event | category | flops | bytes accessed | tf_op | source)
XLA Modules:
  0.0 28.1 jit_solution(7128739489770738445)
XLA Ops:
  0.0 26.5 %shard_map.73 = f32[1,3,96,96]{3,2,1,0:T(8,128)} custom-call(f32[3,96,96]{2,1,0:T(8,128)} %start_hbm.1, f32[1,96,96]{2,1,0:T(8,128)} %mob_hbm.1, bf16[2,192,288]{2,1,0:T(8,128)(2,1)} %constant.10.clone.left_hbm, bf16[2,256,128]{2,1,0:T(8,128)(2,1)} %constant.11.clone.right_hbm, bf16[2,128,256]{2,1,0:T(8,128)(2,1)} %constant.12.clone.back_right_hbm, ...), custom_call_target="tpu_custom_call" | custom-call | flops 200000000 | bytes 1500000 | tf_op jit(solution)/shard_map/pallas_call | solution.py:384
  26.5 1.6 %copy.9 = f32[1,3,96,96]{3,2,1,0:T(8,128)} copy(f32[1,3,96,96]{3,2,1,0:T(8,128)} %shard_map.73) | data formatting | bytes 221184

commit v2 on v1

--- a/solution.py
+++ b/solution.py
@@ -19,7 +19,7 @@
 MEAN = 1.0
 LANES = 128
 ROWS = 8
-PER = 1
+PER = 2
 F32 = jnp.float32
 BF16 = jnp.bfloat16
 
@@ -183,12 +183,25 @@
         load.start()
     barrier = pltpu.get_barrier_semaphore()
 
-    def greet(k, carry):
-        other = lax.rem(me + k, n)
-        pl.semaphore_signal(barrier, inc=1, device_id={"tm": other}, device_id_type=MESH)
-        return carry
-
-    lax.fori_loop(1, n, greet, 0)
+    def scans(index):
+        hit = index == scanners[0]
+        for d in scanners[1:]:
+            hit = jnp.logical_or(hit, index == d)
+        return hit
+
+    one_of = scans(me)
+    greeted = 0
+    for d in range(n):
+        if d in scanners:
+            meets = me != d
+        else:
+            near = jnp.logical_or(me == d - 1, me == d + 1)
+            meets = jnp.logical_or(near, one_of)
+        greeted = greeted + jnp.where(meets, 1, 0)
+
+        @pl.when(meets)
+        def _():
+            pl.semaphore_signal(barrier, inc=1, device_id={"tm": d}, device_id_type=MESH)
 
     lane = lax.broadcasted_iota(jnp.int32, (grid, LANES), 1)
 
@@ -240,13 +253,7 @@
     def drain(ref, sem):
         pltpu.make_async_copy(ref, ref, sem).wait()
 
-    def is_scanner():
-        hit = me == scanners[0]
-        for d in scanners[1:]:
-            hit = jnp.logical_or(hit, me == d)
-        return hit
-
-    def scan(it, start_modes_ref, offsets, inclusive):
+    def send(it, offsets):
         modes[it] = offsets
         for s, d in enumerate(scanners):
             @pl.when(me != d)
@@ -255,6 +262,8 @@
                     modes.at[it, pl.ds(s * per, per)], gathered.at[it, me],
                     send_one.at[it], recv_one.at[it], d,
                 ).start()
+
+    def scan(it, start_modes_ref, inclusive):
         for s, d in enumerate(scanners):
             @pl.when(me == d)
             def _():
@@ -278,8 +287,6 @@
                     state = after
 
     def scanned(it):
-        one_of = is_scanner()
-
         @pl.when(one_of)
         def _():
             drain(returned.at[it, pl.ds(0, (count - 1) * per)], recv_two.at[it])
@@ -305,16 +312,17 @@
     step = [step_ref[k] for k in range(4)]
     start_modes = forward(u0)
     modes[2] = start_modes
-    pl.semaphore_wait(barrier, n - 1)
+    a2 = rate(w)
+    integral = combine((DT / 6.0, f0), (DT * 2.0 / 3.0, a1), (DT / 6.0, a2))
+    offsets = forward(integral) - mode_rate(step, start_modes)
+    pl.semaphore_wait(barrier, greeted)
+    send(0, offsets)
 
     @pl.when(me + 1 < n)
     def _():
         remote(fluct, arrived, w_send, w_recv, me + 1).start()
 
-    a2 = rate(w)
-    integral = combine((DT / 6.0, f0), (DT * 2.0 / 3.0, a1), (DT / 6.0, a2))
-    offsets = forward(integral) - mode_rate(step, start_modes)
-    scan(0, modes.at[2], offsets, False)
+    scan(0, modes.at[2], False)
 
     p0 = block_mean(u0)
     u1f = combine((1.0, u1), (-0.5, p0), (-0.5, pw))
@@ -350,7 +358,8 @@
     a2 = rate(w)
     integral = combine((DT / 6.0, a0), (DT * 2.0 / 3.0, a1), (DT / 6.0, a2))
     offsets = forward(integral) - mode_rate(step, begin)
-    scan(1, modes.at[2], offsets, True)
+    send(1, offsets)
+    scan(1, modes.at[2], True)
     pw = block_mean(w)
     wf = combine((1.0, w), (-1.0, pw))
     for f in range(3):
@@ -363,7 +372,6 @@
     def _():
         drain(fluct, w_send)
 
-    one_of = is_scanner()
     for it in range(2):
         @pl.when(one_of)
         def _():
@@ -380,7 +388,8 @@
     made = constants(grid)
     tiles = made[-1].shape[1]
     count = tiles // PER
-    scanners = tuple(s * n // count for s in range(count))
+    first, width = (n // 4, n // 2) if n // 2 >= count else (0, n)
+    scanners = tuple(first + s * width // count for s in range(count))
     return pl.pallas_call(
         functools.partial(kernel, n, scanners),
         out_shape=jax.ShapeDtypeStruct((1,) + start_state.shape, F32),

time: 28.3 us -> 26 us (0.919)
  Pallas kernels: 26.5 us -> 24.3 us
    pallas_call x1, Pallas kernels: 26.5 us -> 24.3 us  [local(): pl.pallas_call(functools.partial(kernel, n, scanners), out_shape=jax.Shap...]
where the time goes in v2:
time: 26 us; the launch traced here: 25.9 us
  Pallas kernels  24.3 us (93%)
  local copies, waits for them, and re-layouts  1.58 us (6%)
    pallas_call x1, Pallas kernels, local(): pl.pallas_call(functools.partial(kernel, n, scanners), out_shape=jax.Shap...  24.3 us
    unnamed x1, local copies, waits for them, and re-layouts  1.58 us

profile of v2, /device:TPU:0, one launch (start us, length us, event | category | flops | bytes accessed | tf_op | source)
XLA Modules:
  0.0 25.9 jit_solution(4537717144586904173)
XLA Ops:
  0.0 24.3 %shard_map.73 = f32[1,3,96,96]{3,2,1,0:T(8,128)} custom-call(f32[3,96,96]{2,1,0:T(8,128)} %start_hbm.1, f32[1,96,96]{2,1,0:T(8,128)} %mob_hbm.1, bf16[2,192,288]{2,1,0:T(8,128)(2,1)} %constant.10.clone.left_hbm, bf16[2,256,128]{2,1,0:T(8,128)(2,1)} %constant.11.clone.right_hbm, bf16[2,128,256]{2,1,0:T(8,128)(2,1)} %constant.12.clone.back_right_hbm, ...), custom_call_target="tpu_custom_call" | custom-call | flops 200000000 | bytes 1500000 | tf_op jit(solution)/shard_map/pallas_call | solution.py:393
  24.3 1.6 %copy.9 = f32[1,3,96,96]{3,2,1,0:T(8,128)} copy(f32[1,3,96,96]{3,2,1,0:T(8,128)} %shard_map.73) | data formatting | bytes 221184

commit v3 on v2

--- a/solution.py
+++ b/solution.py
@@ -392,7 +392,7 @@
     scanners = tuple(first + s * width // count for s in range(count))
     return pl.pallas_call(
         functools.partial(kernel, n, scanners),
-        out_shape=jax.ShapeDtypeStruct((1,) + start_state.shape, F32),
+        out_shape=pltpu.VMEM((1,) + start_state.shape, F32),
         in_specs=[pl.BlockSpec(memory_space=pl.ANY)] * (2 + len(made)),
         out_specs=pl.BlockSpec(memory_space=pltpu.VMEM),
         scratch_shapes=[pltpu.VMEM(x.shape, x.dtype) for x in (start_state, mobility, *made)]
@@ -413,7 +413,7 @@
             pltpu.SemaphoreType.DMA((2,)),
         ],
         compiler_params=pltpu.CompilerParams(
-            collective_id=0, has_side_effects=True, vmem_limit_bytes=60 * 1024 * 1024
+            collective_id=0, has_side_effects=True, vmem_limit_bytes=56 * 1024 * 1024
         ),
         cost_estimate=pl.CostEstimate(flops=200_000_000, bytes_accessed=1_500_000, transcendentals=0),
     )(start_state, mobility, *[jnp.asarray(m) for m in made])

time: 26 us -> 24.4 us (0.938)
  local copies, waits for them, and re-layouts: 1.58 us -> 0.66 us
  Pallas kernels: 24.3 us -> 23.6 us
    unnamed x1, local copies, waits for them, and re-layouts: 1.58 us -> 0.66 us
    pallas_call x1, Pallas kernels: 24.3 us -> 23.6 us  [local(): pl.pallas_call(functools.partial(kernel, n, scanners), out_shape=pltpu.VM...]
where the time goes in v3:
time: 24.4 us; the launch traced here: 24.3 us
  Pallas kernels  23.6 us (97%)
  local copies, waits for them, and re-layouts  0.66 us (3%)
    pallas_call x1, Pallas kernels, local(): pl.pallas_call(functools.partial(kernel, n, scanners), out_shape=pltpu.VM...  23.6 us
    unnamed x1, local copies, waits for them, and re-layouts  0.66 us

profile of v3, /device:TPU:0, one launch (start us, length us, event | category | flops | bytes accessed | tf_op | source)
XLA Modules:
  0.0 24.3 jit_solution(5076894882161672998)
XLA Ops:
  0.0 23.6 %shard_map.73 = f32[1,3,96,96]{3,2,1,0:T(8,128)S(1)} custom-call(f32[3,96,96]{2,1,0:T(8,128)} %start_hbm.1, f32[1,96,96]{2,1,0:T(8,128)} %mob_hbm.1, bf16[2,192,288]{2,1,0:T(8,128)(2,1)} %constant.10.clone.left_hbm, bf16[2,256,128]{2,1,0:T(8,128)(2,1)} %constant.11.clone.right_hbm, bf16[2,128,256]{2,1,0:T(8,128)(2,1)} %constant.12.clone.back_right_hbm, ...), custom_call_target="tpu_custom_call" | custom-call | flops 200000000 | bytes 1500000 | tf_op jit(solution)/shard_map/pallas_call | solution.py:393
  23.6 0.7 %copy.9 = f32[1,3,96,96]{3,2,1,0:T(8,128)} copy(f32[1,3,96,96]{3,2,1,0:T(8,128)S(1)} %shard_map.73) | data formatting | bytes 221184
